TPU v7x, 256 devices: a whole 4x4x8 slice. The times are simulated.
256 devices in a mesh: dp: 32 (over y_lo, z, core), tensor: 8 (over x, y_hi).
Axes of the slice: x: 4, y: 4 (y_hi: 2, y_lo: 2; y = y_hi * 2 + y_lo), z: 8, core: 2. Of those that a mesh axis runs over, the one named last changes fastest.
Arguments:
- tokens: bfloat16 [32768, 4096], P(('dp', 'tensor')), may hold values from -24 to 24
- out_grad: bfloat16 [32768, 2048], P('dp', 'tensor'), may hold values from -6 to 6
- weights: bfloat16 [4096, 2, 2048], P(None, None, 'tensor'), may hold values from -0.09375 to 0.09375
- master: float32 [4096, 2, 2048], P('dp', None, 'tensor'), may hold values from -0.09375 to 0.09375
- first_moment: float32 [4096, 2, 2048], P('dp', None, 'tensor'), may hold values from -4 to 4
- second_moment: float32 [4096, 2, 2048], P('dp', None, 'tensor'), may hold values from 0.05 to 5
Outputs:
- input_grad: bfloat16 [32768, 4096], P(('dp', 'tensor'))
- new_weights: bfloat16 [4096, 2, 2048], P(None, None, 'tensor')
- new_master: float32 [4096, 2, 2048], P('dp', None, 'tensor')
- new_first: float32 [4096, 2, 2048], P('dp', None, 'tensor')
- new_second: float32 [4096, 2, 2048], P('dp', None, 'tensor')
All inputs are finite; a program needn't handle non-finite values.
Results may differ from a plain program's by a relative error of at most 0.012.
Values may be sent and summed in bfloat16 or wider, within the bound.
No kernel may reach another device: no remote copies, remote signals or barrier semaphores. Data moves between devices by JAX's collectives and lax.ppermute only.
A program may use at most 128 MiB of HBM per device.

v0:
```python
import jax
import jax.numpy as jnp
from jax import lax
from jax.sharding import PartitionSpec as P

SEQ = 512


def linear_step(earlier, latter):
    return (earlier[0] * latter[0], latter[0] * earlier[1] + latter[1])


def local_backward(projected, out_grad):
    token_count = projected.shape[0]
    hidden_width = projected.shape[1] // 2
    shaped = (token_count // SEQ, SEQ, hidden_width)
    gate_value = jax.nn.sigmoid(projected[:, :hidden_width]).reshape(shaped)
    candidate = projected[:, hidden_width:].reshape(shaped)
    upstream = out_grad.astype(jnp.float32).reshape(shaped)
    retain = 1.0 - gate_value
    _, hidden_state = lax.associative_scan(linear_step, (retain, gate_value * candidate), axis=1)
    zeros_row = jnp.zeros_like(hidden_state[:, :1])
    previous = jnp.concatenate([zeros_row, hidden_state[:, :-1]], axis=1)
    retain_next = jnp.concatenate([retain[:, 1:], zeros_row], axis=1)
    _, flipped = lax.associative_scan(
        linear_step, (jnp.flip(retain_next, axis=1), jnp.flip(upstream, axis=1)), axis=1
    )
    adjoint = jnp.flip(flipped, axis=1)
    gate_grad = adjoint * (candidate - previous) * gate_value * retain
    candidate_grad = adjoint * gate_value
    joined = jnp.concatenate([gate_grad, candidate_grad], axis=2)
    return joined.reshape(token_count, 2 * hidden_width).astype(jnp.bfloat16)


def adamw_update(gradient, master, first_moment, second_moment):
    new_first = 0.9 * first_moment + 0.1 * gradient
    new_second = 0.95 * second_moment + 0.05 * gradient * gradient
    update = new_first / (1.0 - 0.9**10) / (jnp.sqrt(new_second / (1.0 - 0.95**10)) + 1e-08)
    new_master = master - 0.001 * (update + 0.1 * master)
    return (new_master, new_first, new_second)


def body(tokens, out_grad, weights, master, first_moment, second_moment):
    model_width = weights.shape[0]
    half_width = weights.shape[2]
    flat_weights = weights.reshape(model_width, 2 * half_width)
    gathered = lax.all_gather(tokens, "tensor", axis=0, tiled=True)
    projected = jnp.dot(gathered, flat_weights, preferred_element_type=jnp.float32)
    pre_grad = local_backward(projected, out_grad)
    replicas = lax.axis_size("dp")
    owner_rows = model_width // replicas
    loss_scale = (gathered.shape[0] * replicas) ** (-0.5)
    input_sum = lax.psum_scatter(
        lax.dot_general(
            pre_grad, flat_weights, (((1,), (1,)), ((), ())), preferred_element_type=jnp.float32
        ).astype(jnp.bfloat16),
        "tensor",
        scatter_dimension=0,
        tiled=True,
    )
    product = lax.dot_general(
        gathered, pre_grad, (((0,), (0,)), ((), ())), preferred_element_type=jnp.float32
    )
    gradient_sum = lax.psum_scatter(
        product.reshape(owner_rows * lax.axis_size("dp"), 2, half_width).astype(jnp.bfloat16),
        "dp",
        scatter_dimension=0,
        tiled=True,
    ).astype(jnp.float32)
    new_master, new_first, new_second = adamw_update(
        gradient_sum * loss_scale, master, first_moment, second_moment
    )
    new_weights = lax.all_gather(new_master.astype(jnp.bfloat16), "dp", axis=0, tiled=True)
    return (input_sum, new_weights, new_master, new_first, new_second)


def solution(mesh):
    return jax.shard_map(
        body,
        mesh=mesh,
        in_specs=(
            P(("dp", "tensor"), None),
            P("dp", "tensor"),
            P(None, None, "tensor"),
            P("dp", None, "tensor"),
            P("dp", None, "tensor"),
            P("dp", None, "tensor"),
        ),
        out_specs=(
            P(("dp", "tensor"), None),
            P(None, None, "tensor"),
            P("dp", None, "tensor"),
            P("dp", None, "tensor"),
            P("dp", None, "tensor"),
        ),
        check_vma=False,
    )
```

profile of v0, /device:TPU:1, one launch (start us, length us, event | category | flops | bytes accessed | tf_op | source)
XLA Modules:
  0.0 834.9 jit_solution(4778969797885212192)
XLA Ops:
  7.9 2.9 slice.452
  10.8 2.9 slice.454
  13.7 2.9 slice.518
  17.9 4.9 copy.13
  22.8 2.6 slice.453
  25.4 2.6 slice.455
  28.0 2.8 slice.519
  30.9 97.2 %all-gather.3.cloned.1.call-done = bf16[1024,4096]{1,0:T(8,128)(2,1)} async-done(((bf16[128,4096]{1,0:T(8,128)(2,1)}), bf16[1024,4096]{1,0:T(8,128)(2,1)}) %all-gather.3.cloned.1.call-update) | async-done | bytes 8388624 | tf_op jit(solution)/shard_map/all_gather | solution.py:47
  128.1 8.1 fusion.51
  137.6 4.1 slice.524
  141.8 4.1 slice.525
  145.9 2.2 slice.523
  148.0 2.1 slice.527
  150.2 2.6 fusion.35
  152.8 1.7 slice.530
  154.5 1.7 slice.531
  156.2 1.7 slice.529
  157.9 1.7 slice.533
  159.6 2.0 fusion.37
  163.0 1.6 slice.535
  164.6 1.6 slice.539
  166.2 1.8 fusion.39
  170.8 1.5 slice.545
  172.4 1.6 fusion.41
  212.5 1.5 slice.540
  216.0 1.6 slice.534
  218.1 1.7 slice.585
  219.9 1.7 slice.528
  222.9 2.2 slice.522
  225.1 4.2 slice.587
  230.7 2.2 slice.450
  232.9 2.2 slice.457
  235.1 4.7 slice.451
  239.8 4.8 slice.458
  244.6 2.7 fusion.36
  247.2 1.7 slice.461
  249.0 1.7 slice.462
  250.7 1.7 slice.460
  252.4 1.7 slice.464
  254.1 2.0 fusion.38
  257.4 1.6 slice.466
  259.0 1.6 slice.470
  260.6 1.8 fusion.40
  265.2 1.5 slice.476
  266.8 1.6 fusion.42
  309.7 1.6 slice.465
  311.9 1.8 slice.516
  313.7 1.7 slice.459
  316.7 2.2 slice.448
  331.8 3.0 pad.258
  336.9 2.0 pad.186
  347.8 2.9 pad.129
  350.8 4.9 slice.449
  359.0 2.3 add.280
  361.4 8.9 %rev.6 = f32[2,512,256]{2,1,0:T(8,128)} reverse(f32[2,512,256]{2,1,0:T(8,128)} %add.280), dimensions={1} | reverse | bytes 2097152 | tf_op jit(solution)/shard_map/jit(_flip)/rev | solution.py:28
  370.2 1.7 slice_add_fusion.4
  374.4 9.8 %convolution_convert_fusion.1 = bf16[512,4096]{1,0:T(8,128)(2,1)} fusion(bf16[1024,512]{1,0:T(8,128)(2,1)S(1)} %bitcast.44, bf16[1024,4096]{1,0:T(8,128)(2,1)} %all-gather.3.cloned.1.call-done), kind=kOutput, calls=%fused_computation.1 | convolution fusion | flops 4297064448 | bytes 13631488 | tf_op jit(solution)/shard_map/dot_general | solution.py:61
  384.2 11.2 %copy.12 = bf16[4096,2,256]{2,1,0:T(2,128)(2,1)} copy(bf16[4096,2,256]{0,2,1:T(8,128)(2,1)} %bitcast.41) | data formatting | bytes 8388608 | tf_op jit(solution)/shard_map/convert_element_type | solution.py:65
  397.3 231.3 %all-reduce.41.cloned.1.call-done = bf16[4096,2,256]{2,1,0:T(2,128)(2,1)} async-done(((bf16[4096,2,256]{2,1,0:T(2,128)(2,1)}), bf16[4096,2,256]{2,1,0:T(2,128)(2,1)}) %all-reduce.41.cloned.1.call-update) | async-done | bytes 4194320
  628.6 2.8 fusion.30
  631.5 9.0 %convolution_convert_fusion = bf16[1024,4096]{1,0:T(8,128)(2,1)} fusion(bf16[4096,512]{1,0:T(8,128)(2,1)} %bitcast.40, bf16[1024,256]{1,0:T(8,128)(2,1)S(1)} %bitcast.43, bf16[1024,256]{1,0:T(8,128)(2,1)S(1)} %bitcast.42), kind=kOutput, calls=%fused_computation | convolution fusion | flops 4301258752 | bytes 13631488 | tf_op jit(solution)/shard_map/dot_general | solution.py:54
  640.5 56.8 %all-gather.5.cloned.1.call-done = bf16[4096,2,256]{2,1,0:T(2,128)(2,1)} async-done(((bf16[128,2,256]{2,1,0:T(2,128)(2,1)}), bf16[4096,2,256]{2,1,0:T(2,128)(2,1)}) %all-gather.5.cloned.1.call-update) | async-done | bytes 4194320 | tf_op jit(solution)/shard_map/all_gather | solution.py:73
  697.4 123.3 %reduce-scatter.2.cloned.1.call-done = bf16[128,4096]{1,0:T(8,128)(2,1)} async-done(((bf16[1024,4096]{1,0:T(8,128)(2,1)}), bf16[128,4096]{1,0:T(8,128)(2,1)}) %reduce-scatter.2.cloned.1.call-update) | async-done | bytes 1048592 | tf_op jit(solution)/shard_map/reduce_scatter | solution.py:53
  820.7 7.7 copy.16
  (213 shorter events, 129.5 us)
Async XLA Ops:
  7.2 120.9 %all-gather.3.cloned.1.call-start = ((), (), s32[]{:S(2)}) async-start(), calls=%async_computation.1 | async-start | bytes 9437184 | tf_op jit(solution)/shard_map/all_gather | solution.py:47
  7.9 620.7 %all-reduce.41.cloned.1.call-start = ((), (), s32[]{:S(2)}) async-start(), calls=%async_computation.4 | async-start | bytes 8388608
  309.0 17.5 %copy-start.8 = (f32[2,63,256]{2,1,0:T(8,128)S(1)}, f32[2,63,256]{2,1,0:T(8,128)}, u32[]{:S(2)}) copy-start(f32[2,63,256]{2,1,0:T(8,128)} %slice.583) | copy-start | bytes 387076
  311.9 17.0 %copy-start.4 = (f32[2,127,256]{2,1,0:T(8,128)S(1)}, f32[2,127,256]{2,1,0:T(8,128)}, u32[]{:S(2)}) copy-start(f32[2,127,256]{2,1,0:T(8,128)} %slice.585) | copy-start | bytes 780292
  318.8 10.1 %copy-start.5 = (f32[2,127,256]{2,1,0:T(8,128)S(1)}, f32[2,127,256]{2,1,0:T(8,128)}, u32[]{:S(2)}) copy-start(f32[2,127,256]{2,1,0:T(8,128)} %slice.528) | copy-start | bytes 780292
  331.8 13.0 %copy-start.11 = (f32[2,31,256]{2,1,0:T(8,128)S(1)}, f32[2,31,256]{2,1,0:T(8,128)}, u32[]{:S(2)}) copy-start(f32[2,31,256]{2,1,0:T(8,128)} %slice.471) | copy-start | bytes 190468
  331.8 13.0 %copy-start.12 = (f32[2,31,256]{2,1,0:T(8,128)S(1)}, f32[2,31,256]{2,1,0:T(8,128)}, u32[]{:S(2)}) copy-start(f32[2,31,256]{2,1,0:T(8,128)} %slice.512) | copy-start | bytes 190468
  334.7 10.9 %copy-start.9 = (f32[2,63,256]{2,1,0:T(8,128)S(1)}, f32[2,63,256]{2,1,0:T(8,128)}, u32[]{:S(2)}) copy-start(f32[2,63,256]{2,1,0:T(8,128)} %slice.514) | copy-start | bytes 387076
  334.7 10.9 %copy-start.10 = (f32[2,63,256]{2,1,0:T(8,128)S(1)}, f32[2,63,256]{2,1,0:T(8,128)}, u32[]{:S(2)}) copy-start(f32[2,63,256]{2,1,0:T(8,128)} %slice.465) | copy-start | bytes 387076
  336.1 10.4 %copy-start.6 = (f32[2,127,256]{2,1,0:T(8,128)S(1)}, f32[2,127,256]{2,1,0:T(8,128)}, u32[]{:S(2)}) copy-start(f32[2,127,256]{2,1,0:T(8,128)} %slice.516) | copy-start | bytes 780292
  336.1 10.4 %copy-start.7 = (f32[2,127,256]{2,1,0:T(8,128)S(1)}, f32[2,127,256]{2,1,0:T(8,128)}, u32[]{:S(2)}) copy-start(f32[2,127,256]{2,1,0:T(8,128)} %slice.459) | copy-start | bytes 780292
  342.5 4.1 copy-start.17
  346.7 10.3 %copy-start.16 = (f32[2,1,256]{2,1,0:T(1,128)S(1)}, f32[2,1,256]{2,1,0:T(1,128)}, u32[]{:S(2)}) copy-start(f32[2,1,256]{2,1,0:T(1,128)} %slice.589) | copy-start | bytes 6148
  373.4 0.8 copy-start
  373.5 1.0 copy-start.2
  395.3 0.7 copy-start.18
  395.3 233.3 %copy-start.13 = (f32[128,2,256]{2,1,0:T(2,128)S(1)}, f32[128,2,256]{2,1,0:T(2,128)}, u32[]{:S(2)}) copy-start(f32[128,2,256]{2,1,0:T(2,128)} %param.9) | copy-start | bytes 786436
  395.3 233.3 %copy-start.14 = (f32[128,2,256]{2,1,0:T(2,128)S(1)}, f32[128,2,256]{2,1,0:T(2,128)}, u32[]{:S(2)}) copy-start(f32[128,2,256]{2,1,0:T(2,128)} %param.10) | copy-start | bytes 786436
  395.3 233.3 %copy-start.15 = (f32[128,2,256]{2,1,0:T(2,128)S(1)}, f32[128,2,256]{2,1,0:T(2,128)}, u32[]{:S(2)}) copy-start(f32[128,2,256]{2,1,0:T(2,128)} %param.11) | copy-start | bytes 786436
  395.4 236.1 %copy-start.1 = (bf16[2,512,256]{2,1,0:T(8,128)(2,1)S(1)}, bf16[2,512,256]{2,1,0:T(8,128)(2,1)}, u32[]{:S(2)}) copy-start(bf16[2,512,256]{2,1,0:T(8,128)(2,1)} %copy-done) | copy-start | bytes 1572868
  395.4 236.1 %copy-start.3 = (bf16[2,512,256]{2,1,0:T(8,128)(2,1)S(1)}, bf16[2,512,256]{2,1,0:T(8,128)(2,1)}, u32[]{:S(2)}) copy-start(bf16[2,512,256]{2,1,0:T(8,128)(2,1)} %copy-done.2) | copy-start | bytes 1572868
  395.4 302.0 %all-gather.5.cloned.1.call-start = ((), (), s32[]{:S(2)}) async-start(), calls=%async_computation.3 | async-start | bytes 4325376 | tf_op jit(solution)/shard_map/all_gather | solution.py:73
  631.4 189.3 %reduce-scatter.2.cloned.1.call-start = ((), (), s32[]{:S(2)}) async-start(), calls=%async_computation.2 | async-start | bytes 9437184 | tf_op jit(solution)/shard_map/reduce_scatter | solution.py:53
Sparse Core Ops, SparseCore 0:
  10.6 117.3 all-gather.2
  395.5 233.0 all-reduce.40
  631.5 65.8 all-gather.4
  702.0 118.6 reduce-scatter.1
where the time goes:
time: 842 us; the launch traced here: 835 us
  waiting for transfers between devices  509 us (60%)
  local copies, waits for them, and re-layouts  220 us (26%)
  other arithmetic  63 us (7%)
  matrix products  27 us (3%)
  between operations  15 us (2%)
    unnamed x5, waiting for transfers between devices  232 us
    reduce_scatter x1, waiting for transfers between devices, body(): lax.psum_scatter(lax.dot_general(pre_grad, flat_weights, (((1,), (1,)), (...  123 us
    all_gather x1, waiting for transfers between devices, body(): gathered = lax.all_gather(tokens, 'tensor', axis=0, tiled=True)  97.2 us
    slice x59, local copies, waits for them, and re-layouts, local_backward(): lax.associative_scan(linear_step, (jnp.flip(retain_next, axis=1), jnp.fli...  95.4 us
    slice x53, local copies, waits for them, and re-layouts, local_backward(): lax.associative_scan(linear_step, (retain, gate_value * candidate), axis=1)  77.4 us
    all_gather x1, waiting for transfers between devices, body(): lax.all_gather(new_master.astype(jnp.bfloat16), 'dp', axis=0, tiled=True)  56.8 us
    mul x14, other arithmetic, linear_step(): return (earlier[0] * latter[0], latter[0] * earlier[1] + latter[1])  24.3 us
    unnamed x42, local copies, waits for them, and re-layouts  17.7 us
  transfers between devices with their start and end apart: 4, of which 4 were waited for; matrix products, arithmetic and copies ran while one was open for 4% of the time, Pallas kernels for 0%

commit v1 on v0

v1 whole, which is shorter than its diff:
```python
import jax, jax.numpy as jnp
from jax import lax
from jax.experimental import pallas as pl
from jax.experimental.pallas import tpu as pltpu
from jax.sharding import PartitionSpec as P

SEQ = 512
GROUP = 8

def scan_kernel(projected_ref, upstream_ref, out_ref, gate_ref, slope_ref):
    width = upstream_ref.shape[1]
    sequences = upstream_ref.shape[0] // SEQ
    row = lax.broadcasted_iota(jnp.int32, (GROUP, width), 0)
    zero = jnp.zeros((GROUP, width), jnp.float32)

    def down(x, k, fill):
        return jnp.where(row >= k, pltpu.roll(x, k, axis=0), fill)

    def up(x, k, fill):
        return jnp.where(row < GROUP - k, pltpu.roll(x, GROUP - k, axis=0), fill)

    def forward(step, carries):
        after = []
        for sequence in range(sequences):
            carry = carries[sequence]
            for half in range(2):
                rows = pl.ds(pl.multiple_of(sequence * SEQ + step * 16, 16) + half * 8, GROUP)
                gate = jax.nn.sigmoid(projected_ref[rows, :width])
                candidate = projected_ref[rows, width:]
                retain = 1.0 - gate
                factor, total = retain, gate * candidate
                for k in (1, 2, 4):
                    total = total + factor * down(total, k, 0.0)
                    factor = factor * down(factor, k, 1.0)
                hidden = total + factor * carry
                previous = jnp.where(row >= 1, pltpu.roll(hidden, 1, axis=0), carry)
                carry = jnp.broadcast_to(hidden[GROUP - 1 :], (GROUP, width))
                gate_ref[rows, :] = gate
                slope_ref[rows, :] = (candidate - previous) * gate * retain
            after.append(carry)
        return tuple(after)

    lax.fori_loop(0, SEQ // 16, forward, (zero,) * sequences, unroll=2)

    def backward(index, carries):
        step = SEQ // 16 - 1 - index
        after = []
        for sequence in range(sequences):
            carry = carries[sequence]
            base = pl.multiple_of(sequence * SEQ + step * 16, 16)
            upstream = upstream_ref[pl.ds(base, 16), :].astype(jnp.float32)
            halves = [None, None]
            for half in (1, 0):
                rows = pl.ds(base + half * 8, GROUP)
                incoming = upstream[half * 8 : half * 8 + 8]
                gate = gate_ref[rows, :]
                retain = 1.0 - gate
                factor, total = retain, retain * incoming
                for k in (1, 2, 4):
                    total = total + factor * up(total, k, 0.0)
                    factor = factor * up(factor, k, 1.0)
                passed = total + factor * carry
                adjoint = incoming + jnp.where(
                    row < GROUP - 1, pltpu.roll(passed, GROUP - 1, axis=0), carry
                )
                carry = jnp.broadcast_to(passed[:1], (GROUP, width))
                halves[half] = (adjoint * slope_ref[rows, :], adjoint * gate)
            after.append(carry)
            out_ref[pl.ds(base, 16), :width] = jnp.concatenate(
                [halves[0][0], halves[1][0]], axis=0
            ).astype(jnp.bfloat16)
            out_ref[pl.ds(base, 16), width:] = jnp.concatenate(
                [halves[0][1], halves[1][1]], axis=0
            ).astype(jnp.bfloat16)
        return tuple(after)

    lax.fori_loop(0, SEQ // 16, backward, (zero,) * sequences, unroll=2)


def local_backward(projected, upstream):
    token_count, width = upstream.shape
    return pl.pallas_call(
        scan_kernel,
        out_shape=jax.ShapeDtypeStruct((token_count, 2 * width), jnp.bfloat16),
        in_specs=[pl.BlockSpec(memory_space=pltpu.VMEM)] * 2,
        out_specs=pl.BlockSpec(memory_space=pltpu.VMEM),
        scratch_shapes=[
            pltpu.VMEM((token_count, width), jnp.float32),
            pltpu.VMEM((token_count, width), jnp.float32),
        ],
        compiler_params=pltpu.CompilerParams(vmem_limit_bytes=16 * 1024 * 1024),
        cost_estimate=pl.CostEstimate(
            flops=60 * token_count * width, bytes_accessed=14 * token_count * width,
            transcendentals=token_count * width,
        ),
    )(projected, upstream)


def adamw_update(gradient, master, first_moment, second_moment):
    new_first = 0.9 * first_moment + 0.1 * gradient
    new_second = 0.95 * second_moment + 0.05 * gradient * gradient
    update = new_first / (1.0 - 0.9**10) / (jnp.sqrt(new_second / (1.0 - 0.95**10)) + 1e-08)
    new_master = master - 0.001 * (update + 0.1 * master)
    return (new_master, new_first, new_second)


def body(tokens, out_grad, weights, master, first_moment, second_moment):
    model_width = weights.shape[0]
    half_width = weights.shape[2]
    flat_weights = weights.reshape(model_width, 2 * half_width)
    gathered = lax.all_gather(tokens, "tensor", axis=0, tiled=True)
    projected = jnp.dot(gathered, flat_weights, preferred_element_type=jnp.float32)
    pre_grad = local_backward(projected, out_grad)
    replicas = lax.axis_size("dp")
    owner_rows = model_width // replicas
    loss_scale = (gathered.shape[0] * replicas) ** (-0.5)
    product = lax.dot_general(
        gathered, pre_grad, (((0,), (0,)), ((), ())), preferred_element_type=jnp.float32
    )
    gradient_sum = lax.psum_scatter(
        product.astype(jnp.bfloat16), "dp", scatter_dimension=0, tiled=True
    )
    gradient_sum = gradient_sum.reshape(owner_rows, 2, half_width).astype(jnp.float32)
    input_sum = lax.psum_scatter(
        lax.dot_general(
            pre_grad, flat_weights, (((1,), (1,)), ((), ())), preferred_element_type=jnp.float32
        ).astype(jnp.bfloat16),
        "tensor",
        scatter_dimension=0,
        tiled=True,
    )
    new_master, new_first, new_second = adamw_update(
        gradient_sum * loss_scale, master, first_moment, second_moment
    )
    new_weights = lax.all_gather(new_master.astype(jnp.bfloat16), "dp", axis=0, tiled=True)
    return (input_sum, new_weights, new_master, new_first, new_second)


def solution(mesh):
    return jax.shard_map(
        body,
        mesh=mesh,
        in_specs=(
            P(("dp", "tensor"), None),
            P("dp", "tensor"),
            P(None, None, "tensor"),
            P("dp", None, "tensor"),
            P("dp", None, "tensor"),
            P("dp", None, "tensor"),
        ),
        out_specs=(
            P(("dp", "tensor"), None),
            P(None, None, "tensor"),
            P("dp", None, "tensor"),
            P("dp", None, "tensor"),
            P("dp", None, "tensor"),
        ),
        check_vma=False,
    )
```

time: 842 us -> 476 us (0.57)
  local copies, waits for them, and re-layouts: 220 us -> 23.9 us
  waiting for transfers between devices: 509 us -> 411 us
  other arithmetic: 63 us -> 0.25 us
    slice x114 -> x0, local copies, waits for them, and re-layouts: 175 us -> none  [the longest x59 95.4 us: local_backward(): lax.associative_scan(linear_step, (jnp.flip(retain_next, axis=1), jnp.fli...]
    unnamed x5, waiting for transfers between devices: 232 us -> 118 us
    mul x15 -> x1, other arithmetic: 25.4 us -> 0.05 us  [adamw_update(): new_second = 0.95 * second_moment + 0.05 * gradient * gradient]
    add x36 -> x0, other arithmetic: 19.8 us -> none  [the longest x18 12 us: linear_step(): return (earlier[0] * latter[0], latter[0] * earlier[1] + latter[1])]
    all_gather x1, waiting for transfers between devices: 97.2 us -> 115 us  [body(): gathered = lax.all_gather(tokens, 'tensor', axis=0, tiled=True)]
    concatenate x17 -> x0, other arithmetic: 10.5 us -> none  [the longest x8 5.52 us: local_backward(): lax.associative_scan(linear_step, (retain, gate_value * candidate), axis=1)]
    convert_element_type x1, local copies, waits for them, and re-layouts: 11.2 us -> 0.78 us  [body(): new_master.astype(jnp.bfloat16)]
    rev x1 -> x0, local copies, waits for them, and re-layouts: 8.86 us -> none  [local_backward(): adjoint = jnp.flip(flipped, axis=1)]
  transfers between devices with their start and end apart: 4 -> 4, of which waited for: 4 -> 4; matrix products, arithmetic and copies ran while one was open for 4% -> 3% of each run, Pallas kernels for 0% -> 0%
where the time goes in v1:
time: 476 us
  waiting for transfers between devices  411 us (86%)
  local copies, waits for them, and re-layouts  23.9 us (5%)
  matrix products  23.5 us (5%)
  between operations  13.9 us (3%)
    reduce_scatter x1, waiting for transfers between devices, body(): lax.psum_scatter(lax.dot_general(pre_grad, flat_weights, (((1,), (1,)), (...  123 us
    unnamed x5, waiting for transfers between devices  118 us
    all_gather x1, waiting for transfers between devices, body(): gathered = lax.all_gather(tokens, 'tensor', axis=0, tiled=True)  115 us
    all_gather x1, waiting for transfers between devices, body(): lax.all_gather(new_master.astype(jnp.bfloat16), 'dp', axis=0, tiled=True)  55.4 us
    unnamed x17, local copies, waits for them, and re-layouts  22.9 us
  transfers between devices with their start and end apart: 4, of which 4 were waited for; matrix products, arithmetic and copies ran while one was open for 3% of the time, Pallas kernels for 0%

profile of v1, /device:TPU:1, one launch (start us, length us, event | category | flops | bytes accessed | tf_op | source)
XLA Modules:
  0.0 475.8 jit_solution(17337494326130750038)
XLA Ops:
  7.2 0.0 all-gather.3.cloned.1.call-start
  7.2 0.7 all-gather.3.cloned.1.call-update
  7.9 0.0 reduce-scatter.7.cloned.1.call-start
  7.9 4.9 %copy.35 = bf16[512,8,2,256]{3,1,2,0:T(8,128)(2,1)} copy(bf16[512,8,2,256]{3,2,1,0:T(2,128)(2,1)} %bitcast.13) | data formatting | bytes 8388608
  12.9 115.2 %all-gather.3.cloned.1.call-done = bf16[1024,4096]{1,0:T(8,128)(2,1)} async-done(((bf16[128,4096]{1,0:T(8,128)(2,1)}), bf16[1024,4096]{1,0:T(8,128)(2,1)}) %all-gather.3.cloned.1.call-update) | async-done | bytes 8388624 | tf_op jit(solution)/shard_map/all_gather | solution.py:111
  128.1 0.0 copy-start
  128.1 0.0 copy-start.4
  128.1 8.3 %fusion.7.projected_ref = f32[1024,512]{1,0:T(8,128)S(1)} fusion(bf16[1024,4096]{1,0:T(8,128)(2,1)} %all-gather.3.cloned.1.call-done, bf16[4096,512]{1,0:T(8,128)(2,1)} %bitcast.14), kind=kOutput, calls=%fused_computation.13 | convolution fusion | flops 4294967296 | bytes 14680064 | tf_op jit(solution)/shard_map/dot_general | solution.py:112
  136.4 0.0 copy-done
  136.4 2.6 shard_map.101
  139.0 0.0 copy-done.4
  139.0 6.3 %fusion = bf16[4096,512]{0,1:T(8,128)(2,1)} fusion(bf16[1024,512]{1,0:T(8,128)(2,1)S(1)} %shard_map.101, bf16[1024,4096]{1,0:T(8,128)(2,1)S(1)} %copy-done.4), kind=kOutput, calls=%fused_computation.2 | convolution fusion | flops 4297064448 | bytes 13631488 | tf_op jit(solution)/shard_map/dot_general | solution.py:117
  145.3 6.5 %copy.33 = bf16[4096,512]{1,0:T(8,128)(2,1)} copy(bf16[4096,512]{0,1:T(8,128)(2,1)} %fusion) | data formatting | bytes 8388608
  151.8 0.0 copy-start.1
  151.8 0.0 copy-start.2
  151.8 0.0 copy-start.3
  151.8 0.0 reduce-scatter.7.cloned.1.call-update
  151.8 0.0 all-gather.5.cloned.1.call-start
  151.9 116.9 %reduce-scatter.7.cloned.1.call-done = bf16[128,512]{1,0:T(8,128)(2,1)} async-done(((bf16[4096,512]{1,0:T(8,128)(2,1)}), bf16[128,512]{1,0:T(8,128)(2,1)}) %reduce-scatter.7.cloned.1.call-update) | async-done | bytes 131088
  268.7 1.0 copy.34
  269.8 0.1 fusion.1
  269.8 0.1 copy.26
  270.0 0.1 copy.24
  270.1 0.0 copy-done.1
  270.1 0.0 copy-done.2
  270.1 0.0 copy-done.3
  270.1 0.2 fusion.4
  270.3 0.8 copy.29
  271.1 0.0 all-gather.5.cloned.1.call-update
  271.1 0.0 reduce-scatter.5.cloned.1.call-start
  271.2 9.0 %convolution_convert_fusion = bf16[1024,4096]{1,0:T(8,128)(2,1)} fusion(bf16[1024,512]{1,0:T(8,128)(2,1)S(1)} %shard_map.101, bf16[4096,512]{1,0:T(8,128)(2,1)} %bitcast.15), kind=kOutput, calls=%fused_computation | convolution fusion | flops 4299161600 | bytes 13631488 | tf_op jit(solution)/shard_map/dot_general | solution.py:125
  280.1 0.0 reduce-scatter.5.cloned.1.call-update
  280.2 0.9 copy.30
  281.1 0.9 copy.31
  282.0 0.9 copy.32
  282.9 55.4 %all-gather.5.cloned.1.call-done = bf16[4096,2,256]{2,1,0:T(2,128)(2,1)} async-done(((bf16[128,2,256]{2,1,0:T(2,128)(2,1)}), bf16[4096,2,256]{2,1,0:T(2,128)(2,1)}) %all-gather.5.cloned.1.call-update) | async-done | bytes 4194320 | tf_op jit(solution)/shard_map/all_gather | solution.py:135
  338.2 123.3 %reduce-scatter.5.cloned.1.call-done = bf16[128,4096]{1,0:T(8,128)(2,1)} async-done(((bf16[1024,4096]{1,0:T(8,128)(2,1)}), bf16[128,4096]{1,0:T(8,128)(2,1)}) %reduce-scatter.5.cloned.1.call-update) | async-done | bytes 1048592 | tf_op jit(solution)/shard_map/reduce_scatter | solution.py:124
  461.6 7.7 %copy.47 = bf16[4096,2,256]{2,1,0:T(2,128)(2,1)} copy(bf16[4096,2,256]{2,1,0:T(2,128)(2,1)} %all-gather.5.cloned.1.call-done) | data formatting | bytes 8388608
Async XLA Ops:
  7.2 120.9 %all-gather.3.cloned.1.call-start = ((), (), s32[]{:S(2)}) async-start(), calls=%async_computation.2 | async-start | bytes 9437184 | tf_op jit(solution)/shard_map/all_gather | solution.py:111
  7.9 260.8 %reduce-scatter.7.cloned.1.call-start = ((), (), s32[]{:S(2)}) async-start(), calls=%async_computation.5 | async-start | bytes 4325376
  128.1 8.3 %copy-start = (bf16[1024,256]{1,0:T(8,128)(2,1)S(1)}, bf16[1024,256]{1,0:T(8,128)(2,1)}, u32[]{:S(2)}) copy-start(bf16[1024,256]{1,0:T(8,128)(2,1)} %upstream_ref.1) | copy-start | bytes 1572868
  128.1 10.9 %copy-start.4 = (bf16[1024,4096]{1,0:T(8,128)(2,1)S(1)}, bf16[1024,4096]{1,0:T(8,128)(2,1)}, u32[]{:S(2)}) copy-start(bf16[1024,4096]{1,0:T(8,128)(2,1)} %all-gather.3.cloned.1.call-done) | copy-start | bytes 25165828
  151.8 118.3 %copy-start.1 = (f32[128,2,256]{2,1,0:T(2,128)S(1)}, f32[128,2,256]{2,1,0:T(2,128)}, u32[]{:S(2)}) copy-start(f32[128,2,256]{2,1,0:T(2,128)} %param.9) | copy-start | bytes 786436
  151.8 118.3 %copy-start.2 = (f32[128,2,256]{2,1,0:T(2,128)S(1)}, f32[128,2,256]{2,1,0:T(2,128)}, u32[]{:S(2)}) copy-start(f32[128,2,256]{2,1,0:T(2,128)} %param.10) | copy-start | bytes 786436
  151.8 118.3 %copy-start.3 = (f32[128,2,256]{2,1,0:T(2,128)S(1)}, f32[128,2,256]{2,1,0:T(2,128)}, u32[]{:S(2)}) copy-start(f32[128,2,256]{2,1,0:T(2,128)} %param.11) | copy-start | bytes 786436
  151.8 186.4 %all-gather.5.cloned.1.call-start = ((), (), s32[]{:S(2)}) async-start(), calls=%async_computation.4 | async-start | bytes 4325376 | tf_op jit(solution)/shard_map/all_gather | solution.py:135
  271.1 190.4 %reduce-scatter.5.cloned.1.call-start = ((), (), s32[]{:S(2)}) async-start(), calls=%async_computation.3 | async-start | bytes 9437184 | tf_op jit(solution)/shard_map/reduce_scatter | solution.py:124
Sparse Core Ops, SparseCore 0:
  10.6 117.3 all-gather.2
  152.0 116.7 reduce-scatter.6
  271.3 66.9 all-gather.4
  342.8 118.7 reduce-scatter.4
